TPU v7x, 128 devices: a whole 4x4x4 slice. The times are simulated.
128 devices in a mesh: node: 16 (over y, z), cls: 8 (over x, core).
Axes of the slice: x: 4, y: 4, z: 4, core: 2. Of those that a mesh axis runs over, the one named last changes fastest.
Arguments:
- seed_scores: float32 [24576, 1024], P('node', 'cls'), may hold values from -6 to 6
- tile_vals: bfloat16 [192, 17, 128, 128], P('node'), may hold values from 0 to 1, as said below
- tile_cols: int32 [192, 17], P('node'), may hold values from 0 to 191, as said below
- tile_count: int32 [192], P('node'), may hold values from 1 to 17, as said below
- tile_scale: float32 [192, 17], P('node'), as said below
Outputs:
- solution: float32 [24576, 1024], P('node', 'cls')
- residual: float32 [24576, 1024], P('node', 'cls')
Inputs may be any that keep to these rules, and one draw needn't show every extreme that they name: `tile_cols`: slot s of block i names block (i + o) mod 192 for an offset o with |o| <= 8, each offset once in a block row; the first tile_count[i] slots hold the tiles present, the diagonal block first. Block i holds a tile of block j exactly when block j holds one of block i, and the two tiles are transposes with equal scales. `tile_count`: some block row holds all 17 tiles. `tile_vals`: tiles on the diagonal block are symmetric. Slots past tile_count hold arbitrary entries. `tile_scale`: every scale lies between 1.2 / (min(128, 16) * 17) and 1.8 / min(128, 16).
All inputs are finite; a program needn't handle non-finite values.
Results may differ from a plain program's by a relative error of at most 0.0065.
The roundings to bfloat16 on the way count: a program that leaves them out, or rounds other values in their place, can miss the bound.
Values may be sent and summed in bfloat16 or wider, within the bound.
A program may use at most 320 MiB of HBM per device.

v0:
```python
import jax
import jax.numpy as jnp
from jax import lax
from jax.sharding import PartitionSpec as P

SHRINK = 0.9
PRECISE = lax.Precision.HIGHEST


def extended(cells, sides, width):
    for axis, dim in sides:
        count = lax.axis_size(axis)
        head = lax.slice_in_dim(cells, 0, width, axis=dim)
        tail = lax.slice_in_dim(cells, cells.shape[dim] - width, cells.shape[dim], axis=dim)
        cells = jnp.concatenate(
            [
                lax.ppermute(tail, axis, [(i, (i + 1) % count) for i in range(count)]),
                cells,
                lax.ppermute(head, axis, [((i + 1) % count, i) for i in range(count)]),
            ],
            axis=dim,
        )
    return cells


def apply_operator(vector, tile_vals, tile_cols, tile_count, tile_scale):
    local_blocks = tile_vals.shape[0]
    slot_total = tile_vals.shape[1]
    tile_size = tile_vals.shape[2]
    reach_blocks = (slot_total - 1) // 2
    width_cols = vector.shape[1]
    blocks_total = local_blocks * lax.axis_size("node")
    first_block = lax.axis_index("node") * local_blocks
    packed = vector.astype(jnp.bfloat16)
    widened = extended(packed, (("node", 0),), reach_blocks * tile_size)
    blocks = widened.reshape(local_blocks + 2 * reach_blocks, tile_size, width_cols)
    placed = jnp.mod(tile_cols - first_block + reach_blocks, blocks_total)
    live_mask = jnp.arange(slot_total)[None, :] < tile_count[:, None]
    weights = jnp.where(live_mask, tile_scale, jnp.zeros_like(tile_scale))
    summed = jnp.zeros((local_blocks, tile_size, width_cols), jnp.float32)
    for slot_index in range(slot_total):
        tiles_now = lax.dynamic_index_in_dim(tile_vals, slot_index, 1, keepdims=False)
        where_now = lax.dynamic_index_in_dim(placed, slot_index, 1, keepdims=False)
        weight_now = lax.dynamic_index_in_dim(weights, slot_index, 1, keepdims=False)
        picked = jnp.take(blocks, where_now, axis=0)
        product = jnp.einsum("bij,bjc->bic", tiles_now, picked, preferred_element_type=jnp.float32)
        summed = summed + weight_now[:, None, None] * product
    return vector - SHRINK * summed.reshape(vector.shape)


def precondition(target, operate):
    estimate = target
    update = target
    factor = SHRINK
    for sweep_index in range(2):
        misfit = target - operate(estimate)
        factor_next = 1.0 / (2.0 / SHRINK - factor)
        update = factor_next * factor * update + 2.0 * factor_next / SHRINK * misfit
        estimate = estimate + update
        factor = factor_next
    return estimate


def body(seed_scores, tile_vals, tile_cols, tile_count, tile_scale):

    def operate(vector):
        return apply_operator(vector, tile_vals, tile_cols, tile_count, tile_scale)

    direction = precondition(seed_scores, operate)
    width_cols = direction.shape[1]
    col_start = lax.axis_index("cls") * width_cols
    imaged = operate(direction)
    all_direction, all_imaged = (
        lax.all_gather(direction, "cls", axis=1, tiled=True),
        lax.all_gather(imaged, "cls", axis=1, tiled=True),
    )
    curvature = jnp.dot(all_direction.T, imaged, precision=PRECISE)
    crossed = jnp.dot(all_direction.T, seed_scores, precision=PRECISE)
    classes_all = all_direction.shape[1]
    blank = jnp.zeros((classes_all, classes_all), jnp.float32)
    padded_curvature = lax.dynamic_update_slice_in_dim(blank, curvature, col_start, 1)
    padded_crossed = lax.dynamic_update_slice_in_dim(blank, crossed, col_start, 1)
    full_curvature, full_crossed = lax.psum((padded_curvature, padded_crossed), ("node", "cls"))
    crossed = lax.dynamic_slice_in_dim(full_crossed, col_start, width_cols, 1)
    lower_factor = jnp.linalg.cholesky(full_curvature)
    coefficients = jax.scipy.linalg.cho_solve((lower_factor, True), crossed)
    solution = jnp.dot(all_direction, coefficients, precision=PRECISE)
    residual = seed_scores - jnp.dot(all_imaged, coefficients, precision=PRECISE)
    return (solution, residual)


def solution(mesh):
    return jax.shard_map(
        body,
        mesh=mesh,
        in_specs=(
            P("node", "cls"),
            P("node", None, None, None),
            P("node", None),
            P("node"),
            P("node", None),
        ),
        out_specs=(P("node", "cls"), P("node", "cls")),
        check_vma=False,
    )
```

profile of v0, /device:TPU:1, one launch (start us, length us, event | category | flops | bytes accessed | tf_op | source)
XLA Modules:
  0.0 709.0 jit_solution(9154764506986143169)
XLA Ops:
  8.4 2.5 collective-permute-start
  11.0 4.7 collective-permute-start.1
  60.9 5.0 collective-permute-start.3
  65.8 5.2 collective-permute-done.2
  111.1 5.2 collective-permute-start.5
  116.2 4.1 collective-permute-done.4
  147.0 2.0 convolution_multiply_fusion.11
  159.3 2.7 broadcast_in_dim.12.clone
  162.0 7.8 %convolution_dynamic-update-slice_fusion = f32[1024,1024]{0,1:T(8,128)} fusion(f32[1024,1024]{0,1:T(8,128)} %broadcast_in_dim.12.clone, s32[]{:T(128)S(6)} %select_n.191, f32[1536,1024]{1,0:T(8,128)} %all-gather.3.cloned.1.call-done, f32[1536,128]{1,0:T(8,128)S(1)} %copy-done.3), kind=kOutput, calls=%fused_computation.112 | convolution fusion | flops 2415919104 | bytes 7602180 | tf_op jit(solution)/shard_map/dot_general | solution.py:78
  169.8 2.5 broadcast_in_dim.12.clone.1
  172.3 4.9 convolution_dynamic-update-slice_fusion.1
  177.9 164.2 %all-reduce.4.cloned.1.call-done = (f32[1024,1024]{0,1:T(8,128)}, f32[1024,1024]{0,1:T(8,128)}) async-done(((f32[1024,1024]{0,1:T(8,128)}, f32[1024,1024]{0,1:T(8,128)}), (f32[1024,1024]{0,1:T(8,128)}, f32[1024,1024]{0,1:T(8,128)})) %all-reduce.4.cloned.1.call-update) | async-done | bytes 8388624 | tf_op jit(solution)/shard_map/psum | solution.py:83
  342.1 5.3 copy.61
  347.4 4.4 fusion
  353.8 11.7 %cholesky.222 = f32[128,128]{1,0:T(8,128)S(1)} custom-call(f32[128,128]{1,0:T(8,128)S(1)} %cholesky.577), custom_call_target="Cholesky" | custom-call | tf_op jit(solution)/shard_map/jit(cholesky)/cholesky | solution.py:85
  365.6 9.8 %custom-call.66 = f32[1,128,128]{1,2,0:T(8,128)S(1)} custom-call(f32[1,128,128]{2,1,0:T(8,128)S(1)} %get-tuple-element.103), custom_call_target="InvertDiagBlocksLowerTriangular" | custom-call | tf_op jit(solution)/shard_map/jit(cholesky)/cholesky | solution.py:85
  378.6 11.7 %cholesky.243 = f32[128,128]{1,0:T(8,128)S(1)} custom-call(f32[128,128]{1,0:T(8,128)S(1)} %cholesky.581), custom_call_target="Cholesky" | custom-call | tf_op jit(solution)/shard_map/jit(cholesky)/cholesky | solution.py:85
  391.1 9.8 %custom-call.67 = f32[1,128,128]{1,2,0:T(8,128)S(1)} custom-call(f32[1,128,128]{2,1,0:T(8,128)S(1)} %get-tuple-element.101), custom_call_target="InvertDiagBlocksLowerTriangular" | custom-call | tf_op jit(solution)/shard_map/jit(cholesky)/cholesky | solution.py:85
  404.0 2.4 convolution_subtract_fusion.2
  406.4 11.7 %cholesky.466 = f32[128,128]{1,0:T(8,128)S(1)} custom-call(f32[128,128]{1,0:T(8,128)S(1)} %cholesky.586), custom_call_target="Cholesky" | custom-call | tf_op jit(solution)/shard_map/jit(cholesky)/cholesky | solution.py:85
  418.9 9.8 %custom-call.68 = f32[1,128,128]{1,2,0:T(8,128)S(1)} custom-call(f32[1,128,128]{2,1,0:T(8,128)S(1)} %get-tuple-element.99), custom_call_target="InvertDiagBlocksLowerTriangular" | custom-call | tf_op jit(solution)/shard_map/jit(cholesky)/cholesky | solution.py:85
  430.0 3.3 convolution_subtract_fusion.3
  433.3 11.7 %cholesky.485 = f32[128,128]{1,0:T(8,128)S(1)} custom-call(f32[128,128]{1,0:T(8,128)S(1)} %cholesky.591), custom_call_target="Cholesky" | custom-call | tf_op jit(solution)/shard_map/jit(cholesky)/cholesky | solution.py:85
  445.8 9.8 %custom-call.69 = f32[1,128,128]{1,2,0:T(8,128)S(1)} custom-call(f32[1,128,128]{2,1,0:T(8,128)S(1)} %get-tuple-element.97), custom_call_target="InvertDiagBlocksLowerTriangular" | custom-call | tf_op jit(solution)/shard_map/jit(cholesky)/cholesky | solution.py:85
  456.7 3.2 convolution_subtract_fusion.4
  459.9 12.1 %cholesky.504 = f32[128,128]{1,0:T(8,128)S(1)} custom-call(f32[128,128]{1,0:T(8,128)S(1)} %cholesky.596), custom_call_target="Cholesky" | custom-call | tf_op jit(solution)/shard_map/jit(cholesky)/cholesky | solution.py:85
  472.8 9.8 %custom-call.70 = f32[1,128,128]{1,2,0:T(8,128)S(1)} custom-call(f32[1,128,128]{2,1,0:T(8,128)S(1)} %get-tuple-element.95), custom_call_target="InvertDiagBlocksLowerTriangular" | custom-call | tf_op jit(solution)/shard_map/jit(cholesky)/cholesky | solution.py:85
  483.7 3.1 convolution_subtract_fusion.5
  486.8 11.7 %cholesky.524 = f32[128,128]{1,0:T(8,128)S(1)} custom-call(f32[128,128]{1,0:T(8,128)S(1)} %cholesky.601), custom_call_target="Cholesky" | custom-call | tf_op jit(solution)/shard_map/jit(cholesky)/cholesky | solution.py:85
  499.3 9.8 %custom-call.71 = f32[1,128,128]{1,2,0:T(8,128)S(1)} custom-call(f32[1,128,128]{2,1,0:T(8,128)S(1)} %get-tuple-element.93), custom_call_target="InvertDiagBlocksLowerTriangular" | custom-call | tf_op jit(solution)/shard_map/jit(cholesky)/cholesky | solution.py:85
  510.1 2.8 convolution_subtract_fusion.6
  512.9 11.7 %cholesky.544 = f32[128,128]{1,0:T(8,128)S(1)} custom-call(f32[128,128]{1,0:T(8,128)S(1)} %cholesky.606), custom_call_target="Cholesky" | custom-call | tf_op jit(solution)/shard_map/jit(cholesky)/cholesky | solution.py:85
  525.4 9.8 %custom-call.72 = f32[1,128,128]{1,2,0:T(8,128)S(1)} custom-call(f32[1,128,128]{2,1,0:T(8,128)S(1)} %get-tuple-element.91), custom_call_target="InvertDiagBlocksLowerTriangular" | custom-call | tf_op jit(solution)/shard_map/jit(cholesky)/cholesky | solution.py:85
  536.1 2.1 convolution_subtract_fusion.17
  538.2 11.7 %cholesky.562 = f32[128,128]{1,0:T(8,128)S(1)} custom-call(f32[128,128]{1,0:T(8,128)S(1)} %convolution_subtract_fusion.17), custom_call_target="Cholesky" | custom-call | tf_op jit(solution)/shard_map/jit(cholesky)/cholesky | solution.py:85
  561.0 4.8 select_select_fusion
  565.8 24.1 %while.1 = (s32[]{:T(128)}, f32[1024,1024]{0,1:T(8,128)}, s32[8,2]{0,1:T(2,128)S(1)}, f32[8,128,128]{2,1,0:T(8,128)S(1)}, s32[]{:T(128)}) while((s32[]{:T(128)}, f32[1024,1024]{0,1:T(8,128)}, s32[8,2]{0,1:T(2,128)S(1)}, f32[8,128,128]{2,1,0:T(8,128)S(1)}, s32[]{:T(128)}) %tuple.106), condition=%wide.while_cond, body=%wide.while_body.sunk | while | flops 2 | bytes 393321 | solution.py:86
  566.4 2.3 dynamic-slice.26
  569.4 2.3 dynamic-slice.26
  572.4 2.3 dynamic-slice.26
  575.5 2.3 dynamic-slice.26
  578.5 2.3 dynamic-slice.26
  581.5 2.3 dynamic-slice.26
  584.5 2.3 dynamic-slice.26
  587.5 2.2 dynamic-slice.26
  589.9 78.8 %custom-call.73 = f32[8,128,128]{1,2,0:T(8,128)S(1)} custom-call(f32[8,128,128]{2,1,0:T(8,128)S(1)} %get-tuple-element.10), custom_call_target="InvertDiagBlocksLowerTriangular" | custom-call | tf_op jit(solution)/shard_map/jit(_cho_solve)/triangular_solve | solution.py:86
  687.7 6.3 fusion.473
  693.9 8.1 %convolution_subtract_fusion = f32[1536,128]{1,0:T(8,128)} fusion(f32[1536,128]{1,0:T(8,128)S(1)} %copy-done.3, f32[1536,1024]{1,0:T(8,128)} %all-gather.5.cloned.1.call-done, f32[1024,128]{1,0:T(8,128)S(1)} %constant_dynamic-update-slice_fusion.36), kind=kOutput, calls=%fused_computation.57 | convolution fusion | flops 2416115712 | bytes 8388608 | tf_op jit(solution)/shard_map/dot_general | solution.py:88
  (445 shorter events, 171.2 us)
Async XLA Ops:
  7.2 152.2 %all-gather.3.cloned.1.call-start = ((), (), s32[]{:S(2)}) async-start(), calls=%async_computation | async-start | bytes 7077888 | tf_op jit(solution)/shard_map/all_gather | solution.py:74
  8.4 14.8 %collective-permute-start = (bf16[1024,128]{1,0:T(8,128)(2,1)S(1)}, bf16[1024,128]{1,0:T(8,128)(2,1)S(1)}, u32[]{:S(2)}, u32[]{:S(2)}) collective-permute-start(bf16[1024,128]{1,0:T(8,128)(2,1)S(1)} %get-tuple-element.71), channel_id=1, source_target_pairs={{0,8},{8,16},{16,24},{24,32},{32,40},{40,48},{48,56},{56,64},{64,7... | collective-permute-start | bytes 786440 | tf_op jit(solution)/shard_map/ppermute | solution.py:17
  11.0 12.3 %collective-permute-start.1 = (bf16[1024,128]{1,0:T(8,128)(2,1)S(1)}, bf16[1024,128]{1,0:T(8,128)(2,1)S(1)}, u32[]{:S(2)}, u32[]{:S(2)}) collective-permute-start(bf16[1024,128]{1,0:T(8,128)(2,1)S(1)} %get-tuple-element.72), channel_id=1, source_target_pairs={{8,0},{16,8},{24,16},{32,24},{40,32},{48,40},{56,48},{64,56},{72,6... | collective-permute-start | bytes 786440 | tf_op jit(solution)/shard_map/ppermute | solution.py:19
  18.9 16.6 %copy-start.50 = (s32[1024]{0:T(1024)}, s32[1024]{0:T(1024)S(1)}, u32[]{:S(2)}) copy-start(s32[1024]{0:T(1024)S(1)} %pad_clamp_fusion.7) | copy-start | bytes 12292
  18.9 16.6 %copy-start.51 = (s32[1024]{0:T(1024)}, s32[1024]{0:T(1024)S(1)}, u32[]{:S(2)}) copy-start(s32[1024]{0:T(1024)S(1)} %pad_clamp_fusion.8) | copy-start | bytes 12292
  19.0 16.6 %copy-start.52 = (s32[1024]{0:T(1024)}, s32[1024]{0:T(1024)S(1)}, u32[]{:S(2)}) copy-start(s32[1024]{0:T(1024)S(1)} %pad_clamp_fusion.9) | copy-start | bytes 12292
  19.0 16.6 %copy-start.53 = (s32[1024]{0:T(1024)}, s32[1024]{0:T(1024)S(1)}, u32[]{:S(2)}) copy-start(s32[1024]{0:T(1024)S(1)} %pad_clamp_fusion.10) | copy-start | bytes 12292
  19.0 16.6 %copy-start.54 = (s32[1024]{0:T(1024)}, s32[1024]{0:T(1024)S(1)}, u32[]{:S(2)}) copy-start(s32[1024]{0:T(1024)S(1)} %pad_clamp_fusion.11) | copy-start | bytes 12292
  19.0 16.6 %copy-start.55 = (s32[1024]{0:T(1024)}, s32[1024]{0:T(1024)S(1)}, u32[]{:S(2)}) copy-start(s32[1024]{0:T(1024)S(1)} %pad_clamp_fusion.12) | copy-start | bytes 12292
  19.1 16.5 %copy-start.56 = (s32[1024]{0:T(1024)}, s32[1024]{0:T(1024)S(1)}, u32[]{:S(2)}) copy-start(s32[1024]{0:T(1024)S(1)} %pad_clamp_fusion.13) | copy-start | bytes 12292
  37.0 18.2 %slice-start = ((s8[6684672]{0:T(1024)(128)(4,1)}), s8[2490368]{0:T(1024)(128)(4,1)S(1)}, s32[]{:S(2)}) async-start(s8[6684672]{0:T(1024)(128)(4,1)} %bitcast.388), calls=%async_computation.3 | async-start | bytes 4980736
  47.4 4.9 copy-start.48
  47.4 6.3 copy-start.45
  47.5 7.7 %copy-start.43 = (bf16[12,128,128]{2,1,0:T(8,128)(2,1)S(1)}, bf16[12,128,128]{2,1,0:T(8,128)(2,1)}, u32[]{:S(2)}) copy-start(bf16[12,128,128]{2,1,0:T(8,128)(2,1)} %gather_fusion.7) | copy-start | bytes 1179652
  47.5 7.7 %slice-start.1 = ((s8[6684672]{0:T(1024)(128)(4,1)}), s8[4194304]{0:T(1024)(128)(4,1)S(1)}, s32[]{:S(2)}) async-start(s8[6684672]{0:T(1024)(128)(4,1)} %bitcast.388), calls=%async_computation.4 | async-start | bytes 8388608
  49.1 6.4 copy-start.40
  50.8 5.1 copy-start.38
  52.3 3.9 copy-start.34
  53.7 2.9 copy-start.32
  60.6 10.5 %copy-start.8 = (f32[12,128,128]{2,1,0:T(8,128)}, f32[12,128,128]{2,1,0:T(8,128)S(1)}, u32[]{:S(2)}) copy-start(f32[12,128,128]{2,1,0:T(8,128)S(1)} %fusion.21) | copy-start | bytes 2359300
  60.8 10.2 %collective-permute-start.2 = (bf16[1024,128]{1,0:T(8,128)(2,1)S(1)}, bf16[1024,128]{1,0:T(8,128)(2,1)S(1)}, u32[]{:S(2)}, u32[]{:S(2)}) collective-permute-start(bf16[1024,128]{1,0:T(8,128)(2,1)S(1)} %get-tuple-element.69), channel_id=1, source_target_pairs={{0,8},{8,16},{16,24},{24,32},{32,40},{40,48},{48,56},{56,64},{64,7... | collective-permute-start | bytes 786440 | tf_op jit(solution)/shard_map/ppermute | solution.py:17
  60.9 10.2 %collective-permute-start.3 = (bf16[1024,128]{1,0:T(8,128)(2,1)S(1)}, bf16[1024,128]{1,0:T(8,128)(2,1)S(1)}, u32[]{:S(2)}, u32[]{:S(2)}) collective-permute-start(bf16[1024,128]{1,0:T(8,128)(2,1)S(1)} %get-tuple-element.70), channel_id=1, source_target_pairs={{8,0},{16,8},{24,16},{32,24},{40,32},{48,40},{56,48},{64,56},{72,6... | collective-permute-start | bytes 786440 | tf_op jit(solution)/shard_map/ppermute | solution.py:19
  84.0 19.6 %slice-start.2 = ((s8[6684672]{0:T(1024)(128)(4,1)}), s8[2490368]{0:T(1024)(128)(4,1)S(1)}, s32[]{:S(2)}) async-start(s8[6684672]{0:T(1024)(128)(4,1)} %bitcast.390), calls=%async_computation.5 | async-start | bytes 4980736
  96.0 6.3 copy-start.49
  96.0 7.7 %slice-start.3 = ((s8[6684672]{0:T(1024)(128)(4,1)}), s8[4194304]{0:T(1024)(128)(4,1)S(1)}, s32[]{:S(2)}) async-start(s8[6684672]{0:T(1024)(128)(4,1)} %bitcast.390), calls=%async_computation.6 | async-start | bytes 8388608
  96.0 7.7 %copy-start.47 = (bf16[12,128,128]{2,1,0:T(8,128)(2,1)S(1)}, bf16[12,128,128]{2,1,0:T(8,128)(2,1)}, u32[]{:S(2)}) copy-start(bf16[12,128,128]{2,1,0:T(8,128)(2,1)} %gather_fusion.24) | copy-start | bytes 1179652
  97.6 6.5 copy-start.46
  99.2 5.2 copy-start.44
  100.8 4.0 copy-start.42
  102.3 2.9 copy-start.41
  110.9 231.2 %all-reduce.4.cloned.1.call-start = ((), (), s32[]{:S(2)}) async-start(), calls=%async_computation.2 | async-start | bytes 16777216 | tf_op jit(solution)/shard_map/psum | solution.py:83
  111.0 9.3 %collective-permute-start.4 = (bf16[1024,128]{1,0:T(8,128)(2,1)S(1)}, bf16[1024,128]{1,0:T(8,128)(2,1)S(1)}, u32[]{:S(2)}, u32[]{:S(2)}) collective-permute-start(bf16[1024,128]{1,0:T(8,128)(2,1)S(1)} %get-tuple-element.67), channel_id=1, source_target_pairs={{0,8},{8,16},{16,24},{24,32},{32,40},{40,48},{48,56},{56,64},{64,7... | collective-permute-start | bytes 786440 | tf_op jit(solution)/shard_map/ppermute | solution.py:17
  111.1 9.2 %collective-permute-start.5 = (bf16[1024,128]{1,0:T(8,128)(2,1)S(1)}, bf16[1024,128]{1,0:T(8,128)(2,1)S(1)}, u32[]{:S(2)}, u32[]{:S(2)}) collective-permute-start(bf16[1024,128]{1,0:T(8,128)(2,1)S(1)} %get-tuple-element.68), channel_id=1, source_target_pairs={{8,0},{16,8},{24,16},{32,24},{40,32},{48,40},{56,48},{64,56},{72,6... | collective-permute-start | bytes 786440 | tf_op jit(solution)/shard_map/ppermute | solution.py:19
  133.4 20.1 %slice-start.4 = ((s8[6684672]{0:T(1024)(128)(4,1)}), s8[2490368]{0:T(1024)(128)(4,1)S(1)}, s32[]{:S(2)}) async-start(s8[6684672]{0:T(1024)(128)(4,1)} %bitcast.392), calls=%async_computation.7 | async-start | bytes 4980736
  145.4 6.7 copy-start.26
  145.4 8.1 %slice-start.5 = ((s8[6684672]{0:T(1024)(128)(4,1)}), s8[4194304]{0:T(1024)(128)(4,1)S(1)}, s32[]{:S(2)}) async-start(s8[6684672]{0:T(1024)(128)(4,1)} %bitcast.392), calls=%async_computation.8 | async-start | bytes 8388608
  145.4 8.1 %copy-start.25 = (bf16[12,128,128]{2,1,0:T(8,128)(2,1)S(1)}, bf16[12,128,128]{2,1,0:T(8,128)(2,1)}, u32[]{:S(2)}) copy-start(bf16[12,128,128]{2,1,0:T(8,128)(2,1)} %gather_fusion.35) | copy-start | bytes 1179652
  147.0 6.9 copy-start.24
  149.0 5.2 copy-start.23
  150.5 4.0 copy-start.22
  152.1 2.9 copy-start.21
  159.3 13.0 %copy-start.6 = (f32[1536,128]{1,0:T(8,128)}, f32[1536,128]{1,0:T(8,128)S(1)}, u32[]{:S(2)}) copy-start(f32[1536,128]{1,0:T(8,128)S(1)} %bitcast_subtract_fusion) | copy-start | bytes 2359300
  159.3 13.0 %slice-start.6 = ((s8[6291456]{0:T(1024)(128)(4,1)}), s8[4194304]{0:T(1024)(128)(4,1)S(1)}, s32[]{:S(2)}) async-start(s8[6291456]{0:T(1024)(128)(4,1)} %bitcast.394), calls=%async_computation.9 | async-start | bytes 8388608
  162.0 10.3 %slice-start.7 = ((s8[6291456]{0:T(1024)(128)(4,1)}), s8[2097152]{0:T(1024)(128)(4,1)S(1)}, s32[]{:S(2)}) async-start(s8[6291456]{0:T(1024)(128)(4,1)} %bitcast.394), calls=%async_computation.10 | async-start | bytes 4194304
  177.2 516.7 %all-gather.5.cloned.1.call-start = ((), (), s32[]{:S(2)}) async-start(), calls=%async_computation.1 | async-start | bytes 7077888 | tf_op jit(solution)/shard_map/all_gather | solution.py:75
  668.7 10.1 %copy-start.4 = (f32[1024,1024]{0,1:T(8,128)S(1)}, f32[1024,1024]{0,1:T(8,128)}, u32[]{:S(2)}) copy-start(f32[1024,1024]{0,1:T(8,128)} %get-tuple-element.203) | copy-start | bytes 12582916
  672.8 14.9 %slice-start.8 = ((s8[6291456]{0:T(1024)(128)(4,1)}), s8[4194304]{0:T(1024)(128)(4,1)S(1)}, s32[]{:S(2)}) async-start(s8[6291456]{0:T(1024)(128)(4,1)} %bitcast.396), calls=%async_computation.11 | async-start | bytes 8388608
  684.0 3.7 slice-start.9
  (31 other events, 49.5 us)
Sparse Core Ops, SparseCore 0:
  111.0 47.4 all-gather.2
  177.3 164.7 all-reduce.3
  343.9 43.9 all-gather.4
where the time goes:
time: 718 us; the launch traced here: 709 us
  other arithmetic  266 us (37%)
  waiting for transfers between devices  174 us (24%)
  local copies, waits for them, and re-layouts  123 us (17%)
  matrix products  107 us (15%)
  between operations  21.4 us (3%)
  starting transfers between devices  17.6 us (2%)
    another operation x31, other arithmetic, body(): lower_factor = jnp.linalg.cholesky(full_curvature)  168 us
    psum x1, waiting for transfers between devices, body(): lax.psum((padded_curvature, padded_crossed), ('node', 'cls'))  164 us
    another operation x3, other arithmetic, body(): coefficients = jax.scipy.linalg.cho_solve((lower_factor, True), crossed)  83.6 us
    gather x51, local copies, waits for them, and re-layouts, apply_operator(): picked = jnp.take(blocks, where_now, axis=0)  74 us
    dot_general x51, matrix products, apply_operator(): jnp.einsum('bij,bjc->bic', tiles_now, picked, preferred_element_type=jnp....  36.2 us
    another operation x14, matrix products, body(): lower_factor = jnp.linalg.cholesky(full_curvature)  25.9 us
    another operation x40, local copies, waits for them, and re-layouts  23.8 us
    another operation x30, matrix products, body(): coefficients = jax.scipy.linalg.cho_solve((lower_factor, True), crossed)  18.4 us
  transfers between devices with their start and end apart: 9, of which 3 were waited for; matrix products, arithmetic and copies ran while one was open for 55% of the time, Pallas kernels for 0%

commit v1 on v0

v1 whole, which is shorter than its diff:
```python
import functools
import jax
import jax.numpy as jnp
from jax import lax
from jax.experimental import pallas as pl
from jax.experimental.pallas import tpu as pltpu
from jax.sharding import PartitionSpec as P

SHRINK = 0.9
HI = lax.Precision.HIGHEST
MESH = pl.DeviceIdType.MESH
T = 128


def remote(src, dst, send, recv, to):
    return pltpu.make_async_remote_copy(
        src_ref=src, dst_ref=dst, send_sem=send, recv_sem=recv, device_id=to, device_id_type=MESH)


def greet(peers):
    barrier = pltpu.get_barrier_semaphore()
    for peer in peers:
        pl.semaphore_signal(barrier, inc=1, device_id=peer, device_id_type=MESH)
    pl.semaphore_wait(barrier, len(peers))


def direction_kernel(slot_ref, weight_ref, seed_ref, tiles_ref,
                     d_ref, r_ref, image_ref, high_ref, ct_ref, xt_ref,
                     ext_ref, acc_ref, z_ref, low_ref, flat_ref,
                     halo_send, halo_recv, ring_send, ring_recv, pair_send, pair_recv):
    blocks = acc_ref.shape[0] // T
    reach = 8
    rows = blocks * T
    half = rows // 2
    edge = reach * T
    node, cls = lax.axis_index("node"), lax.axis_index("cls")
    nodes = lax.axis_size("node")
    chips = lax.axis_size("cls") // 2
    chip, core = cls // 2, cls % 2
    right_node, left_node = {"node": (node + 1) % nodes}, {"node": (node + nodes - 1) % nodes}
    right_chip, left_chip, far_chip = (chip + 1) % chips, (chip + chips - 1) % chips, (chip + 2) % chips
    right, left, twin = {"cls": right_chip * 2 + core}, {"cls": left_chip * 2 + core}, {"cls": chip * 2 + 1 - core}
    greet([right_node, left_node, right, left, twin])

    def halo_copies(s):
        ext = ext_ref.at[s]
        return (
            remote(ext.at[pl.ds(rows, edge)], ext.at[pl.ds(0, edge)],
                   halo_send.at[s, 0], halo_recv.at[s, 0], right_node),
            remote(ext.at[pl.ds(edge, edge)], ext.at[pl.ds(edge + rows, edge)],
                   halo_send.at[s, 1], halo_recv.at[s, 1], left_node),
        )

    def product(s, tile, source):
        return jnp.dot(tiles_ref[tile], ext_ref[s, pl.ds(pl.multiple_of(source * T, T), T), :],
                       preferred_element_type=jnp.float32)

    def spread(s, z):
        ext_ref[s, edge:edge + rows, :] = z.astype(jnp.bfloat16)
        copies = halo_copies(s)
        for copy in copies:
            copy.start()
        return copies

    def local_part(s):
        def one(i, _):
            total = jnp.zeros((T, T), jnp.float32)
            for j in range(blocks):
                o = j + reach - i
                fits = (o >= 0) & (o <= 2 * reach)
                at = i * (2 * reach + 1) + jnp.clip(o, 0, 2 * reach)
                w = jnp.where(fits, weight_ref[at], 0.0)
                total += w * product(s, slot_ref[at], j + reach)
            acc_ref[pl.ds(pl.multiple_of(i * T, T), T), :] = total
            return 0
        lax.fori_loop(0, blocks, one, 0)

    def edge_part(s):
        def one(t, _):
            low = jnp.zeros((T, T), jnp.float32)
            high = jnp.zeros((T, T), jnp.float32)
            for m in range(reach + 1):
                lower = m < reach - t
                i = jnp.where(lower, t, t + blocks - reach)
                j = t + m + jnp.where(lower, 0, blocks)
                at = i * (2 * reach + 1) + j - i
                w = weight_ref[at]
                p = product(s, slot_ref[at], j)
                low += jnp.where(lower, w, 0.0) * p
                high += jnp.where(lower, 0.0, w) * p
            acc_ref[pl.ds(pl.multiple_of(t * T, T), T), :] += low
            acc_ref[pl.ds(pl.multiple_of((t + blocks - reach) * T, T), T), :] += high
            return 0
        lax.fori_loop(0, reach, one, 0)

    def operate(s, copies):
        local_part(s)
        for copy in copies:
            copy.wait_recv()
        edge_part(s)

    factor = SHRINK
    z_ref[...] = seed_ref[...]
    d_ref[...] = seed_ref[...]
    for s in range(2):
        copies = spread(s, z_ref[...])
        operate(s, copies)
        factor_next = 1.0 / (2.0 / SHRINK - factor)
        misfit = seed_ref[...] - (z_ref[...] - SHRINK * acc_ref[...])
        update = factor_next * factor * d_ref[...] + (2.0 * factor_next / SHRINK) * misfit
        d_ref[...] = update
        z_ref[...] = z_ref[...] + update
        factor = factor_next
        for copy in copies:
            copy.wait_send()
    z = z_ref[...]
    d_ref[...] = z
    high = z.astype(jnp.bfloat16)
    high_ref[cls] = high
    low_ref[cls] = (z - high.astype(jnp.float32)).astype(jnp.bfloat16)
    copies = spread(2, z)

    def ring_copy(q, n, owner, part, to):
        ref = (high_ref, low_ref)[q].at[owner, pl.ds(part * half, half)]
        return remote(ref, ref, ring_send.at[q, n], ring_recv.at[q, n], to)

    def twin_copy(q, n, owner):
        ref = (high_ref, low_ref)[q].at[owner]
        return remote(ref, ref, pair_send.at[q, n], pair_recv.at[q, n], twin)

    first = []
    for q in range(2):
        first.append((ring_copy(q, 0, cls, 0, right), ring_copy(q, 1, cls, 1, left),
                      ring_copy(q, 2, cls, 1, right), ring_copy(q, 3, cls, 0, left)))
        for copy in first[q]:
            copy.start()
    own = [twin_copy(q, 0, cls) for q in range(2)]
    for copy in own:
        copy.start()
    operate(2, copies)
    image_ref[...] = z_ref[...] - SHRINK * acc_ref[...]
    r_ref[...] = seed_ref[...] - image_ref[...]

    image_t = image_ref[...].T
    r_t = r_ref[...].T
    for n, value in enumerate((image_t, r_t)):
        top = value.astype(jnp.bfloat16)
        flat_ref[n * T:(n + 1) * T, :] = top
        flat_ref[(2 + n) * T:(3 + n) * T, :] = (value - top.astype(jnp.float32)).astype(jnp.bfloat16)

    second = []
    for q in range(2):
        first[q][0].wait_recv()
        a = ring_copy(q, 4, left_chip * 2 + core, 0, right)
        a.start()
        first[q][1].wait_recv()
        b = ring_copy(q, 5, right_chip * 2 + core, 1, left)
        b.start()
        second.append((a, b))
        first[q][2].wait_recv()
        c = twin_copy(q, 1, left_chip * 2 + core)
        c.start()
        first[q][3].wait_recv()
        d = twin_copy(q, 2, right_chip * 2 + core)
        d.start()
        own.extend((c, d))

    def grams(q, which):
        g = (high_ref, low_ref)[q]
        both = jnp.concatenate([g[which * 2], g[which * 2 + 1]], axis=1)
        at = pl.ds(pl.multiple_of(which * 2 * T, 2 * T), 2 * T)
        if q == 0:
            out = jnp.dot(flat_ref[...], both, preferred_element_type=jnp.float32)
            ct_ref[:, at] = out[0:T] + out[2 * T:3 * T]
            xt_ref[:, at] = out[T:2 * T] + out[3 * T:]
        else:
            out = jnp.dot(flat_ref[0:2 * T, :], both, preferred_element_type=jnp.float32)
            ct_ref[:, at] += out[0:T]
            xt_ref[:, at] += out[T:]

    for q in range(2):
        own[q].wait_recv()
        grams(q, chip)
    far = []
    for q in range(2):
        for copy in second[q]:
            copy.wait_recv()
        e = twin_copy(q, 3, far_chip * 2 + core)
        e.start()
        far.append(e)
        own[2 + 2 * q].wait_recv()
        grams(q, left_chip)
        own[3 + 2 * q].wait_recv()
        grams(q, right_chip)
    for q in range(2):
        far[q].wait_recv()
        grams(q, far_chip)
    for copy in list(copies) + list(first[0]) + list(first[1]) + list(second[0]) + list(second[1]) + own + far:
        copy.wait_send()


def find_direction(slots, weights, seed, tiles):
    rows, width = seed.shape
    every = lax.axis_size("cls")
    f32 = jnp.float32
    vmem = pl.BlockSpec(memory_space=pltpu.VMEM)
    smem = pl.BlockSpec(memory_space=pltpu.SMEM)
    sems = pltpu.SemaphoreType.DMA
    return pl.pallas_call(
        direction_kernel,
        out_shape=[
            jax.ShapeDtypeStruct((rows, width), f32),
            jax.ShapeDtypeStruct((rows, width), f32),
            jax.ShapeDtypeStruct((rows, width), f32),
            jax.ShapeDtypeStruct((every, rows, width), jnp.bfloat16),
            jax.ShapeDtypeStruct((width, every * width), f32),
            jax.ShapeDtypeStruct((width, every * width), f32),
        ],
        in_specs=[smem, smem, vmem, vmem],
        out_specs=[vmem] * 6,
        scratch_shapes=[
            pltpu.VMEM((3, rows + 16 * T, width), jnp.bfloat16),
            pltpu.VMEM((rows, width), f32),
            pltpu.VMEM((rows, width), f32),
            pltpu.VMEM((every, rows, width), jnp.bfloat16),
            pltpu.VMEM((4 * T, rows), jnp.bfloat16),
            sems((3, 2)), sems((3, 2)), sems((2, 6)), sems((2, 6)), sems((2, 4)), sems((2, 4)),
        ],
        compiler_params=pltpu.CompilerParams(collective_id=0, has_side_effects=True, vmem_limit_bytes=48 << 20),
    )(slots, weights, seed, tiles)


def by_offset(tile_cols, tile_count, tile_scale):
    local_blocks, slot_total = tile_cols.shape
    reach = (slot_total - 1) // 2
    total = local_blocks * lax.axis_size("node")
    row = jnp.arange(local_blocks)[:, None]
    where = jnp.mod(tile_cols - (lax.axis_index("node") * local_blocks + row) + reach, total)
    slot = jnp.arange(slot_total)[None, :]
    weights = jnp.where(slot < tile_count[:, None], tile_scale, 0.0)
    hit = where[:, :, None] == jnp.arange(slot_total)[None, None, :]
    slots = jnp.sum(jnp.where(hit, (row * slot_total + slot)[:, :, None], 0), axis=1)
    return slots.reshape(-1), jnp.sum(jnp.where(hit, weights[:, :, None], 0.0), axis=1).reshape(-1)


def dot(a, b, dims=((1,), (0,))):
    return lax.dot_general(a, b, (dims, ((), ())), precision=HI, preferred_element_type=jnp.float32)

def row_of(x, j):
    return jnp.broadcast_to(x[j:j + 1, :], (8, T))

def factor(rows):
    lane = lax.broadcasted_iota(jnp.int32, (8, T), 1)
    sub = lax.broadcasted_iota(jnp.int32, (8, T), 0)
    out = []
    for k in range(16):
        cols = [[jnp.broadcast_to(r[:, 8 * k + j:8 * k + j + 1], (8, T)) for j in range(8)] for r in rows[k:]]
        inside = (lane >= 8 * k) & (lane < 8 * k + 8)
        unit = jnp.where(lane - 8 * k == sub, 1.0, 0.0)
        panel = jnp.where(inside, unit, rows[k])
        b = list(cols[0])
        done = jnp.zeros((8, T), jnp.float32)
        for j in range(8):
            p = row_of(b[j], j)
            r = 1.0 / p
            f = b[j]
            own = sub == j
            top = row_of(panel, j)
            done = jnp.where(own, top * lax.rsqrt(p), done)
            n = top * r
            panel = jnp.where(own, n, panel - f * n)
            for l in range(j + 1, 8):
                n = row_of(b[l], j) * r
                b[l] = jnp.where(own, n, b[l] - f * n)
        out.append(jnp.where(lane < 8 * k + 8, done, 0.0))
        spread = [row_of(panel, j) for j in range(8)]
        for g in range(k + 1, 16):
            acc = jnp.where(inside, 0.0, rows[g])
            for j in range(8):
                acc = acc - cols[g - k][j] * spread[j]
            rows[g] = acc
    return out

def solve_kernel(c_ref, x_ref, z_ref, a_ref, l_ref, v_ref):
    n = c_ref.shape[0]
    nb = n // T
    for i in range(nb):
        for j in range(i, nb):
            a_ref[i * T:(i + 1) * T, j * T:(j + 1) * T] = 0.5 * (
                c_ref[i * T:(i + 1) * T, j * T:(j + 1) * T] + c_ref[j * T:(j + 1) * T, i * T:(i + 1) * T].T)
    a_ref[:, n:] = x_ref[...]

    def step(k, _):
        base = pl.multiple_of(k * T, T)
        here = pl.ds(base, T)
        rows = [a_ref[pl.ds(base + 8 * g, 8), here] for g in range(16)]
        rows = factor(rows)
        for g in range(16):
            l_ref[pl.ds(base + 8 * g, 8), :] = rows[g]
        v_ref[here, :] = dot(l_ref[here, :], a_ref[here, :])
        def trail(i, _):
            at = pl.multiple_of(i * T, T)
            a_ref[pl.ds(at, T), :] -= dot(v_ref[here, pl.ds(at, T)], v_ref[here, :], ((0,), (0,)))
            return 0
        lax.fori_loop(k + 1, nb, trail, 0)
        return 0
    lax.fori_loop(0, nb, step, 0)
    def back(s, _):
        j = nb - 1 - s
        at = pl.multiple_of(j * T, T)
        known = dot(l_ref[pl.ds(at, T), :], v_ref[pl.ds(at, T), n:], ((0,), (0,)))
        z_ref[pl.ds(at, T), :] = known
        def one(i, _):
            to = pl.multiple_of(i * T, T)
            v_ref[pl.ds(to, T), n:] -= dot(v_ref[pl.ds(to, T), pl.ds(at, T)], known)
            return 0
        lax.fori_loop(0, j, one, 0)
        return 0
    lax.fori_loop(0, nb, back, 0)

def solve(c, x):
    n = c.shape[0]
    return pl.pallas_call(
        solve_kernel,
        out_shape=jax.ShapeDtypeStruct(x.shape, jnp.float32),
        in_specs=[pl.BlockSpec(memory_space=pltpu.VMEM)] * 2,
        out_specs=pl.BlockSpec(memory_space=pltpu.VMEM),
        scratch_shapes=[pltpu.VMEM((n, n + T), jnp.float32), pltpu.VMEM((n, T), jnp.float32),
                        pltpu.VMEM((n, n + T), jnp.float32)],
        compiler_params=pltpu.CompilerParams(vmem_limit_bytes=40 << 20),
    )(c, x)


def body(seed_scores, tile_vals, tile_cols, tile_count, tile_scale):
    slots, weights = by_offset(tile_cols, tile_count, tile_scale)
    tiles = tile_vals.reshape(-1, T, T)
    direction, misfit, imaged, high, ct, xt = find_direction(slots, weights, seed_scores, tiles)
    all_imaged = lax.all_gather(imaged, "cls", axis=1, tiled=True)
    ct, xt = lax.psum((ct, xt), "node")
    full = lax.all_gather(ct, "cls", axis=0, tiled=True)
    start = lax.axis_index("cls") * T
    mine = lax.dynamic_slice_in_dim(full, start, T, 1)
    rhs = (xt + 0.5 * (ct - mine.T)).T
    change = solve(full, rhs)
    packed = change.astype(jnp.bfloat16)
    mixed = sum(jnp.dot(high[n], packed[n * T:(n + 1) * T], preferred_element_type=jnp.float32) for n in range(high.shape[0]))
    solution = direction + mixed
    residual = misfit - jnp.dot(all_imaged, change, precision=HI)
    return (solution, residual)


def solution(mesh):
    return jax.shard_map(
        body,
        mesh=mesh,
        in_specs=(
            P("node", "cls"),
            P("node", None, None, None),
            P("node", None),
            P("node"),
            P("node", None),
        ),
        out_specs=(P("node", "cls"), P("node", "cls")),
        check_vma=False,
    )
```

time: 718 us -> 284 us (0.40); the launches traced: 709 us -> 283 us
  other arithmetic: 266 us -> 3.15 us
  Pallas kernels: 0 us -> 134 us
  local copies, waits for them, and re-layouts: 123 us -> 5.9 us
  matrix products: 107 us -> 11 us
  waiting for transfers between devices: 174 us -> 115 us
  starting transfers between devices: 17.6 us -> 0.3 us
  between operations: 21.4 us -> 13.9 us
    another operation x34 -> x0, other arithmetic: 252 us -> none  [the longest x31 168 us: body(): lower_factor = jnp.linalg.cholesky(full_curvature)]
    pallas_call x0 -> x2, Pallas kernels: none -> 134 us  [the longest x1 69.6 us: solve(): pl.pallas_call(solve_kernel, out_shape=jax.ShapeDtypeStruct(x.shape, jnp....]
    psum x1, waiting for transfers between devices: 164 us -> 81.9 us  [body(): ct, xt = lax.psum((ct, xt), 'node')]
    gather x51 -> x0, local copies, waits for them, and re-layouts: 74 us -> none  [apply_operator(): picked = jnp.take(blocks, where_now, axis=0)]
    dot_general x55 -> x9, matrix products: 63.2 us -> 11 us  [the longest x1 8.11 us: body(): residual = misfit - jnp.dot(all_imaged, change, precision=HI)]
    another operation x44 -> x0, matrix products: 44.2 us -> none  [the longest x14 25.9 us: body(): lower_factor = jnp.linalg.cholesky(full_curvature)]
    all_gather x2, waiting for transfers between devices: 0.02 us -> 32.8 us  [the longest x1 32.8 us: body(): full = lax.all_gather(ct, 'cls', axis=0, tiled=True)]
    another operation x70 -> x0, local copies, waits for them, and re-layouts: 29.7 us -> none
  transfers between devices with their start and end apart: 9 -> 3, of which waited for: 3 -> 2; matrix products, arithmetic and copies ran while one was open for 55% -> 2% of each run, Pallas kernels for 0% -> 25%
where the time goes in v1:
time: 284 us; the launch traced here: 283 us
  Pallas kernels  134 us (47%)
  waiting for transfers between devices  115 us (40%)
  between operations  13.9 us (5%)
  matrix products  11 us (4%)
  local copies, waits for them, and re-layouts  5.9 us (2%)
  other arithmetic  3.15 us (1%)
    psum x1, waiting for transfers between devices, body(): ct, xt = lax.psum((ct, xt), 'node')  81.9 us
    pallas_call x1, Pallas kernels, solve(): pl.pallas_call(solve_kernel, out_shape=jax.ShapeDtypeStruct(x.shape, jnp....  69.6 us
    pallas_call x1, Pallas kernels, find_direction(): pl.pallas_call(direction_kernel, out_shape=[jax.ShapeDtypeStruct((rows, w...  64.2 us
    all_gather x1, waiting for transfers between devices, body(): full = lax.all_gather(ct, 'cls', axis=0, tiled=True)  32.8 us
    dot_general x1, matrix products, body(): residual = misfit - jnp.dot(all_imaged, change, precision=HI)  8.11 us
  transfers between devices with their start and end apart: 3, of which 2 were waited for; matrix products, arithmetic and copies ran while one was open for 2% of the time, Pallas kernels for 25%

profile of v1, /device:TPU:1, one launch (start us, length us, event | category | flops | bytes accessed | tf_op | source)
XLA Modules:
  0.0 283.1 jit_solution(1999376031091007178)
XLA Ops:
  7.2 0.0 all-reduce.3.cloned.1.call-start
  7.3 0.8 add_select_fusion
  8.0 0.1 copy.9
  8.1 0.1 select_reduce_fusion.1
  8.3 0.1 reshape.46.slot_ref
  8.4 0.8 fusion.29
  9.1 0.1 copy.10
  9.2 0.1 select_reduce_fusion
  9.4 0.1 reshape.47.weight_ref
  9.5 0.0 copy-start.1
  9.5 1.1 copy-done.1
  10.6 64.2 %shard_map.68 = (f32[1536,128]{1,0:T(8,128)S(1)}, f32[1536,128]{1,0:T(8,128)S(1)}, f32[1536,128]{1,0:T(8,128)}, bf16[8,1536,128]{2,1,0:T(8,128)(2,1)}, f32[128,1024]{1,0:T(8,128)}, /*index=5*/f32[128,1024]{1,0:T(8,128)S(1)}) custom-call(s32[204]{0:T(256)S(1)} %reshape.46.slot_ref, f32[204]{0:T(256)S(1)} %reshape.47.weight_ref, f32[1536,128]{1,0:T(8,128)S(1)} %copy-done.1, ...), custom_call_target="tpu_custom_call" | custom-call | tf_op jit(solution)/shard_map/pallas_call | solution.py:209
  74.8 1.0 copy.11
  75.8 0.0 all-reduce.3.cloned.1.call-update
  75.8 0.0 all-gather.3.cloned.1.call-start
  75.8 81.9 %all-reduce.3.cloned.1.call-done = (f32[128,1024]{1,0:T(8,128)}, f32[128,1024]{0,1:T(8,128)}) async-done(((f32[128,1024]{1,0:T(8,128)}, f32[128,1024]{0,1:T(8,128)}), (f32[128,1024]{1,0:T(8,128)}, f32[128,1024]{0,1:T(8,128)})) %all-reduce.3.cloned.1.call-update) | async-done | bytes 1048592 | tf_op jit(solution)/shard_map/psum | solution.py:339
  157.7 0.0 all-gather.3.cloned.1.call-update
  157.8 0.2 all-gather.5.cloned.1.call-start
  158.0 0.5 all-gather.5.cloned.1.call-update
  158.5 1.2 copy.12
  159.7 32.8 %all-gather.3.cloned.1.call-done.c_ref = f32[1024,1024]{1,0:T(8,128)} async-done(((f32[128,1024]{1,0:T(8,128)}), f32[1024,1024]{1,0:T(8,128)}) %all-gather.3.cloned.1.call-update) | async-done | bytes 4194320 | tf_op jit(solution)/shard_map/all_gather | solution.py:340
  192.5 1.3 fusion.3.x_ref
  193.8 0.0 copy-start
  193.8 2.2 copy-done
  196.0 0.0 copy-start.2
  196.0 69.6 %shard_map.69 = f32[1024,128]{1,0:T(8,128)S(1)} custom-call(f32[1024,1024]{1,0:T(8,128)S(1)} %copy-done, f32[1024,128]{1,0:T(8,128)S(1)} %fusion.3.x_ref), custom_call_target="tpu_custom_call" | custom-call | tf_op jit(solution)/shard_map/pallas_call | solution.py:323
  265.6 0.0 copy-done.2
  265.6 0.2 fusion.11
  265.9 0.2 convolution_add_fusion.6
  266.1 0.2 convolution_add_fusion.5
  266.4 0.2 convolution_add_fusion.4
  266.6 0.2 convolution_add_fusion.3
  266.9 0.2 convolution_add_fusion.2
  267.1 0.2 convolution_add_fusion.1
  267.4 1.1 fusion
  268.5 0.0 all-gather.5.cloned.1.call-done
  268.5 8.1 %convolution_subtract_fusion = f32[1536,128]{1,0:T(8,128)} fusion(f32[1536,128]{1,0:T(8,128)S(1)} %get-tuple-element.12, f32[1536,1024]{1,0:T(8,128)} %all-gather.5.cloned.1.call-done, f32[1024,128]{1,0:T(8,128)S(1)} %shard_map.69), kind=kOutput, calls=%fused_computation | convolution fusion | flops 2416115712 | bytes 8388608 | tf_op jit(solution)/shard_map/dot_general | solution.py:348
  (4 shorter events, 0.0 us)
Async XLA Ops:
  7.2 150.6 %all-reduce.3.cloned.1.call-start = ((), (), s32[]{:S(2)}) async-start(), calls=%async_computation.2 | async-start | bytes 2097152 | tf_op jit(solution)/shard_map/psum | solution.py:339
  9.5 1.1 copy-start.1
  75.8 116.7 %all-gather.3.cloned.1.call-start = ((), (), s32[]{:S(2)}) async-start(), calls=%async_computation | async-start | bytes 4718592 | tf_op jit(solution)/shard_map/all_gather | solution.py:340
  157.8 110.7 %all-gather.5.cloned.1.call-start = ((), (), s32[]{:S(2)}) async-start(), calls=%async_computation.1 | async-start | bytes 7077888 | tf_op jit(solution)/shard_map/all_gather | solution.py:338
  193.8 2.2 copy-start
  196.0 69.6 %copy-start.2 = (bf16[8,1536,128]{2,1,0:T(8,128)(2,1)S(1)}, bf16[8,1536,128]{2,1,0:T(8,128)(2,1)}, u32[]{:S(2)}) copy-start(bf16[8,1536,128]{2,1,0:T(8,128)(2,1)} %get-tuple-element.9) | copy-start | bytes 9437188
Sparse Core Ops, SparseCore 0:
  75.9 81.7 all-reduce.2
  159.5 33.0 all-gather.2
  194.2 44.9 all-gather.4

commit v2 on v1

--- a/solution.py
+++ b/solution.py
@@ -241,6 +241,128 @@
     hit = where[:, :, None] == jnp.arange(slot_total)[None, None, :]
     slots = jnp.sum(jnp.where(hit, (row * slot_total + slot)[:, :, None], 0), axis=1)
     return slots.reshape(-1), jnp.sum(jnp.where(hit, weights[:, :, None], 0.0), axis=1).reshape(-1)
+
+
+def sum_kernel(ct_ref, xt_ref, full_ref, xs_ref,
+               first_ref, part_ref, second_ref,
+               send1, recv1, send2, recv2, send_a, recv_a, send_b, recv_b, send_c, recv_c,
+               send_t, recv_t, send_xb, recv_xb, send_xc, recv_xc):
+    side = 4
+    node, cls = lax.axis_index("node"), lax.axis_index("cls")
+    chip, core = cls // 2, cls % 2
+    y, z = node // side, node % side
+    f = jnp.where(core == 0, z, y)
+    s = jnp.where(core == 0, y, z)
+
+    def at(f_, s_):
+        return {"node": jnp.where(core == 0, s_ * side + f_, f_ * side + s_)}
+
+    def turn(v, m):
+        return (v + m) % side
+
+    along_f = [at(turn(f, m), s) for m in range(1, side)]
+    along_s = [at(f, turn(s, m)) for m in range(1, side)]
+    along_x = [{"cls": turn(chip, m) * 2 + core} for m in range(1, side)]
+    twin = {"cls": chip * 2 + 1 - core}
+    greet(along_f + along_s + along_x + [twin])
+
+    pending = []
+
+    def go(copies):
+        for copy in copies:
+            copy.start()
+        pending.extend(copies)
+        return copies
+
+    grams = (ct_ref, xt_ref)
+    stage1 = [go([remote(grams[q].at[:, turn(f, m)], first_ref.at[q, m - 1],
+                         send1.at[q, m - 1], recv1.at[q, m - 1], along_f[m - 1])
+                  for m in range(1, side)]) for q in range(2)]
+    stage2 = []
+    for q in range(2):
+        for copy in stage1[q]:
+            copy.wait_recv()
+        for k in range(side):
+            part_ref[q, k] = (grams[q][k, f] + first_ref[q, 0, k]) + (first_ref[q, 1, k] + first_ref[q, 2, k])
+        stage2.append(go([remote(part_ref.at[q, turn(s, m)], second_ref.at[q, m - 1],
+                                 send2.at[q, m - 1], recv2.at[q, m - 1], along_s[m - 1])
+                          for m in range(1, side)]))
+    def finish(q):
+        for copy in stage2[q]:
+            copy.wait_recv()
+        return (part_ref[q, s] + second_ref[q, 0]) + (second_ref[q, 1] + second_ref[q, 2])
+
+    full_ref[chip, core, s, f] = finish(0)
+    mine = full_ref.at[chip, core, s, f]
+    stage_a = go([remote(mine, mine, send_a.at[m], recv_a.at[m], along_x[m]) for m in range(side - 1)])
+    xs_ref[s, f] = finish(1)
+    mine_x = xs_ref.at[s, f]
+    stage_xb = go([remote(mine_x, mine_x, send_xb.at[m], recv_xb.at[m], along_f[m]) for m in range(side - 1)])
+    for copy in stage_a:
+        copy.wait_recv()
+    line = full_ref.at[:, core, s, f]
+    stage_b = go([remote(line, line, send_b.at[m], recv_b.at[m], along_f[m]) for m in range(side - 1)])
+    for copy in stage_xb:
+        copy.wait_recv()
+    line_x = xs_ref.at[s]
+    stage_xc = go([remote(line_x, line_x, send_xc.at[m], recv_xc.at[m], along_s[m]) for m in range(side - 1)])
+    for copy in stage_b:
+        copy.wait_recv()
+
+    def slab(owner, h):
+        return full_ref.at[pl.ds(2 * h, 2), core, owner]
+
+    def ring(n, owner, h, to):
+        return remote(slab(owner, h), slab(owner, h), send_c.at[n], recv_c.at[n], to)
+
+    def share(n, owner, h):
+        return remote(slab(owner, h), slab(owner, h), send_t.at[n], recv_t.at[n], twin)
+
+    up, down = along_s[0], along_s[2]
+    before, after, across = turn(s, 3), turn(s, 1), turn(s, 2)
+    c0, c1, c2, c3 = go([ring(0, s, 0, up), ring(1, s, 1, down), ring(2, s, 1, up), ring(3, s, 0, down)])
+    shared = go([share(0, s, 0), share(1, s, 1)])
+    c0.wait_recv()
+    fwd0, = go([ring(4, before, 0, up)])
+    c1.wait_recv()
+    fwd1, = go([ring(5, after, 1, down)])
+    shared += go([share(2, before, 0), share(3, after, 1)])
+    c2.wait_recv()
+    shared += go([share(4, before, 1)])
+    c3.wait_recv()
+    shared += go([share(5, after, 0)])
+    fwd0.wait_recv()
+    shared += go([share(6, across, 0)])
+    fwd1.wait_recv()
+    shared += go([share(7, across, 1)])
+    for copy in stage_xc + shared:
+        copy.wait_recv()
+    for copy in pending:
+        copy.wait_send()
+
+
+def sum_and_share(ct, xt):
+    width, classes = ct.shape
+    f32 = jnp.float32
+    vmem = pl.BlockSpec(memory_space=pltpu.VMEM)
+    sems = pltpu.SemaphoreType.DMA
+    cut = (4, 4, width // 16, classes)
+    full, xs = pl.pallas_call(
+        sum_kernel,
+        out_shape=[jax.ShapeDtypeStruct((4, 2) + cut, f32), jax.ShapeDtypeStruct(cut, f32)],
+        in_specs=[vmem] * 2,
+        out_specs=[vmem] * 2,
+        scratch_shapes=[
+            pltpu.VMEM((2, 3, 4, width // 16, classes), f32),
+            pltpu.VMEM((2, 4, width // 16, classes), f32),
+            pltpu.VMEM((2, 3, width // 16, classes), f32),
+            sems((2, 3)), sems((2, 3)), sems((2, 3)), sems((2, 3)),
+            sems((3,)), sems((3,)), sems((3,)), sems((3,)), sems((6,)), sems((6,)),
+            sems((8,)), sems((8,)), sems((3,)), sems((3,)), sems((3,)), sems((3,)),
+        ],
+        compiler_params=pltpu.CompilerParams(collective_id=1, has_side_effects=True, vmem_limit_bytes=32 << 20),
+    )(ct.reshape(cut), xt.reshape(cut))
+    return full.reshape(classes, classes), xs.reshape(width, classes)
 
 
 def dot(a, b, dims=((1,), (0,))):
@@ -329,26 +451,22 @@
                         pltpu.VMEM((n, n + T), jnp.float32)],
         compiler_params=pltpu.CompilerParams(vmem_limit_bytes=40 << 20),
     )(c, x)
-
-
 def body(seed_scores, tile_vals, tile_cols, tile_count, tile_scale):
     slots, weights = by_offset(tile_cols, tile_count, tile_scale)
     tiles = tile_vals.reshape(-1, T, T)
     direction, misfit, imaged, high, ct, xt = find_direction(slots, weights, seed_scores, tiles)
     all_imaged = lax.all_gather(imaged, "cls", axis=1, tiled=True)
-    ct, xt = lax.psum((ct, xt), "node")
-    full = lax.all_gather(ct, "cls", axis=0, tiled=True)
+    full, xt = sum_and_share(ct, xt)
     start = lax.axis_index("cls") * T
     mine = lax.dynamic_slice_in_dim(full, start, T, 1)
-    rhs = (xt + 0.5 * (ct - mine.T)).T
+    own = lax.dynamic_slice_in_dim(full, start, T, 0)
+    rhs = (xt + 0.5 * (own - mine.T)).T
     change = solve(full, rhs)
     packed = change.astype(jnp.bfloat16)
     mixed = sum(jnp.dot(high[n], packed[n * T:(n + 1) * T], preferred_element_type=jnp.float32) for n in range(high.shape[0]))
     solution = direction + mixed
     residual = misfit - jnp.dot(all_imaged, change, precision=HI)
     return (solution, residual)
-
-
 def solution(mesh):
     return jax.shard_map(
         body,

time: 284 us -> 210 us (0.74)
  waiting for transfers between devices: 115 us -> 0.02 us
  Pallas kernels: 134 us -> 174 us
    psum x1 -> x0, waiting for transfers between devices: 81.9 us -> none  [body(): ct, xt = lax.psum((ct, xt), 'node')]
    pallas_call x0 -> x1, Pallas kernels: none -> 40.6 us  [sum_and_share(): pl.pallas_call(sum_kernel, out_shape=[jax.ShapeDtypeStruct((4, 2) + cut,...]
    all_gather x1 -> x0, waiting for transfers between devices: 32.8 us -> none  [body(): full = lax.all_gather(ct, 'cls', axis=0, tiled=True)]
  transfers between devices with their start and end apart: 3 -> 1, of which waited for: 2 -> 0; matrix products, arithmetic and copies ran while one was open for 2% -> 3% of each run, Pallas kernels for 25% -> 53%
where the time goes in v2:
time: 210 us
  Pallas kernels  174 us (83%)
  between operations  14.2 us (7%)
  matrix products  11 us (5%)
  local copies, waits for them, and re-layouts  7.14 us (3%)
  other arithmetic  3 us (1%)
    pallas_call x1, Pallas kernels, solve(): pl.pallas_call(solve_kernel, out_shape=jax.ShapeDtypeStruct(x.shape, jnp....  69.7 us
    pallas_call x1, Pallas kernels, find_direction(): pl.pallas_call(direction_kernel, out_shape=[jax.ShapeDtypeStruct((rows, w...  64 us
    pallas_call x1, Pallas kernels, sum_and_share(): pl.pallas_call(sum_kernel, out_shape=[jax.ShapeDtypeStruct((4, 2) + cut,...  40.6 us
    dot_general x1, matrix products, body(): residual = misfit - jnp.dot(all_imaged, change, precision=HI)  8.11 us
    unnamed x8, local copies, waits for them, and re-layouts  5.32 us
  transfers between devices with their start and end apart: 1, of which 0 were waited for; matrix products, arithmetic and copies ran while one was open for 3% of the time, Pallas kernels for 53%

profile of v2, /device:TPU:1, one launch (start us, length us, event | category | flops | bytes accessed | tf_op | source)
XLA Modules:
  0.0 209.6 jit_solution(6814431274885094836)
XLA Ops:
  7.2 0.0 all-gather.2.cloned.1.call-start
  7.3 0.8 add_select_fusion
  8.0 0.1 copy.11
  8.1 0.1 select_reduce_fusion.1
  8.3 0.1 reshape.58.slot_ref
  8.4 0.8 fusion.29
  9.1 0.1 copy.12
  9.2 0.1 select_reduce_fusion
  9.4 0.1 reshape.59.weight_ref
  9.5 0.0 copy-start.2
  9.5 1.1 copy-done.2
  10.6 64.0 %shard_map.68 = (f32[1536,128]{1,0:T(8,128)S(1)}, f32[1536,128]{1,0:T(8,128)S(1)}, f32[1536,128]{1,0:T(8,128)}, bf16[8,1536,128]{2,1,0:T(8,128)(2,1)}, f32[128,1024]{1,0:T(8,128)S(1)}, /*index=5*/f32[128,1024]{1,0:T(8,128)S(1)}) custom-call(s32[204]{0:T(256)S(1)} %reshape.58.slot_ref, f32[204]{0:T(256)S(1)} %reshape.59.weight_ref, ...), custom_call_target="tpu_custom_call" | custom-call | tf_op jit(solution)/shard_map/pallas_call | solution.py:209
  74.6 0.0 all-gather.2.cloned.1.call-update
  74.6 40.6 %shard_map.69 = (f32[4,2,4,4,8,1024]{5,4,3,2,1,0:T(8,128)S(1)}, f32[4,4,8,1024]{3,2,1,0:T(8,128)S(1)}) custom-call(f32[4,4,8,1024]{3,2,1,0:T(8,128)S(1)} %bitcast.44, f32[4,4,8,1024]{3,2,1,0:T(8,128)S(1)} %bitcast.45), custom_call_target="tpu_custom_call" | custom-call | tf_op jit(solution)/shard_map/pallas_call | solution.py:350
  115.2 0.0 copy-start
  115.2 2.0 copy-done
  117.2 0.2 copy.14
  117.4 1.1 constant_dynamic-slice_fusion
  118.5 0.2 copy.13
  118.7 1.1 fusion.3.x_ref
  119.8 0.0 copy-start.1
  119.8 2.2 %copy-done.1 = f32[4,2,4,4,8,1024]{5,4,3,2,1,0:T(8,128)S(1)} copy-done((f32[4,2,4,4,8,1024]{5,4,3,2,1,0:T(8,128)S(1)}, f32[4,2,4,4,8,1024]{5,4,3,2,1,0:T(8,128)}, u32[]{:S(2)}) %copy-start.1) | copy-done | bytes 4194328
  122.0 0.0 copy-start.3
  122.0 69.7 %shard_map.70 = f32[1024,128]{1,0:T(8,128)S(1)} custom-call(f32[1024,1024]{1,0:T(8,128)S(1)} %bitcast.43, f32[1024,128]{1,0:T(8,128)S(1)} %fusion.3.x_ref), custom_call_target="tpu_custom_call" | custom-call | tf_op jit(solution)/shard_map/pallas_call | solution.py:445
  191.8 0.0 copy-done.3
  191.8 0.2 fusion.11
  192.0 0.2 convolution_add_fusion.6
  192.3 0.2 convolution_add_fusion.5
  192.5 0.2 convolution_add_fusion.4
  192.8 0.2 convolution_add_fusion.3
  193.0 0.2 convolution_add_fusion.2
  193.3 0.2 convolution_add_fusion.1
  193.5 1.1 fusion
  194.7 0.0 all-gather.2.cloned.1.call-done
  194.7 8.1 %convolution_subtract_fusion = f32[1536,128]{1,0:T(8,128)} fusion(f32[1536,128]{1,0:T(8,128)S(1)} %get-tuple-element.16, f32[1536,1024]{1,0:T(8,128)} %all-gather.2.cloned.1.call-done, f32[1024,128]{1,0:T(8,128)S(1)} %shard_map.70), kind=kOutput, calls=%fused_computation | convolution fusion | flops 2416115712 | bytes 8388608 | tf_op jit(solution)/shard_map/dot_general | solution.py:468
  (4 shorter events, 0.0 us)
Async XLA Ops:
  7.2 187.5 %all-gather.2.cloned.1.call-start = ((), (), s32[]{:S(2)}) async-start(), calls=%async_computation | async-start | bytes 7077888 | tf_op jit(solution)/shard_map/all_gather | solution.py:458
  9.5 1.1 copy-start.2
  115.2 2.0 copy-start
  119.8 2.2 %copy-start.1 = (f32[4,2,4,4,8,1024]{5,4,3,2,1,0:T(8,128)S(1)}, f32[4,2,4,4,8,1024]{5,4,3,2,1,0:T(8,128)}, u32[]{:S(2)}) copy-start(f32[4,2,4,4,8,1024]{5,4,3,2,1,0:T(8,128)} %copy-done) | copy-start | bytes 12582916
  122.0 69.8 %copy-start.3 = (bf16[8,1536,128]{2,1,0:T(8,128)(2,1)S(1)}, bf16[8,1536,128]{2,1,0:T(8,128)(2,1)}, u32[]{:S(2)}) copy-start(bf16[8,1536,128]{2,1,0:T(8,128)(2,1)} %get-tuple-element.11) | copy-start | bytes 9437188
Sparse Core Ops, SparseCore 0:
  74.7 42.7 all-gather.1

commit v3 on v2

--- a/solution.py
+++ b/solution.py
@@ -25,7 +25,7 @@
 
 
 def direction_kernel(slot_ref, weight_ref, seed_ref, tiles_ref,
-                     d_ref, r_ref, image_ref, high_ref, ct_ref, xt_ref,
+                     d_ref, r_ref, parts_ref, high_ref, ct_ref, xt_ref,
                      ext_ref, acc_ref, z_ref, low_ref, flat_ref,
                      halo_send, halo_recv, ring_send, ring_recv, pair_send, pair_recv):
     blocks = acc_ref.shape[0] // T
@@ -138,10 +138,13 @@
     for copy in own:
         copy.start()
     operate(2, copies)
-    image_ref[...] = z_ref[...] - SHRINK * acc_ref[...]
-    r_ref[...] = seed_ref[...] - image_ref[...]
-
-    image_t = image_ref[...].T
+    image = z_ref[...] - SHRINK * acc_ref[...]
+    r_ref[...] = seed_ref[...] - image
+    coarse = image.astype(jnp.bfloat16)
+    parts_ref[0:rows, :] = coarse
+    parts_ref[rows:, :] = (image - coarse.astype(jnp.float32)).astype(jnp.bfloat16)
+
+    image_t = image.T
     r_t = r_ref[...].T
     for n, value in enumerate((image_t, r_t)):
         top = value.astype(jnp.bfloat16)
@@ -211,7 +214,7 @@
         out_shape=[
             jax.ShapeDtypeStruct((rows, width), f32),
             jax.ShapeDtypeStruct((rows, width), f32),
-            jax.ShapeDtypeStruct((rows, width), f32),
+            jax.ShapeDtypeStruct((2 * rows, width), jnp.bfloat16),
             jax.ShapeDtypeStruct((every, rows, width), jnp.bfloat16),
             jax.ShapeDtypeStruct((width, every * width), f32),
             jax.ShapeDtypeStruct((width, every * width), f32),
@@ -365,6 +368,8 @@
     return full.reshape(classes, classes), xs.reshape(width, classes)
 
 
+ND = 2
+
 def dot(a, b, dims=((1,), (0,))):
     return lax.dot_general(a, b, (dims, ((), ())), precision=HI, preferred_element_type=jnp.float32)
 
@@ -374,99 +379,129 @@
 def factor(rows):
     lane = lax.broadcasted_iota(jnp.int32, (8, T), 1)
     sub = lax.broadcasted_iota(jnp.int32, (8, T), 0)
+    own = [sub == j for j in range(8)]
     out = []
+
+    def splat(x, c):
+        return jnp.broadcast_to(x[:, c:c + 1], (8, T))
+
+    ahead = [splat(rows[0], c) for c in range(8)]
     for k in range(16):
-        cols = [[jnp.broadcast_to(r[:, 8 * k + j:8 * k + j + 1], (8, T)) for j in range(8)] for r in rows[k:]]
+        last = k == 15
         inside = (lane >= 8 * k) & (lane < 8 * k + 8)
-        unit = jnp.where(lane - 8 * k == sub, 1.0, 0.0)
-        panel = jnp.where(inside, unit, rows[k])
-        b = list(cols[0])
+        b = ahead
+        later = [] if last else [splat(rows[k], 8 * k + 8 + c) for c in range(8)]
+        cols = [[splat(r, 8 * k + j) for j in range(8)] for r in rows[k + 1:k + 1 + ND]]
+        fresh = [] if last else [splat(rows[k + 1], 8 * k + 8 + c) for c in range(8)]
+        panel = jnp.where(inside, jnp.where(lane - 8 * k == sub, 1.0, 0.0), rows[k])
         done = jnp.zeros((8, T), jnp.float32)
         for j in range(8):
             p = row_of(b[j], j)
             r = 1.0 / p
             f = b[j]
-            own = sub == j
-            top = row_of(panel, j)
-            done = jnp.where(own, top * lax.rsqrt(p), done)
-            n = top * r
-            panel = jnp.where(own, n, panel - f * n)
+
+            def clear(x):
+                n = row_of(x, j) * r
+                return jnp.where(own[j], n, x - f * n)
+
+            done = jnp.where(own[j], row_of(panel, j) * lax.rsqrt(p), done)
             for l in range(j + 1, 8):
-                n = row_of(b[l], j) * r
-                b[l] = jnp.where(own, n, b[l] - f * n)
+                b[l] = clear(b[l])
+            later = [clear(x) for x in later]
+            panel = clear(panel)
         out.append(jnp.where(lane < 8 * k + 8, done, 0.0))
+        if last:
+            break
+        ahead = []
+        for c in range(8):
+            terms = [cols[0][j] * row_of(later[c], j) for j in range(8)]
+            while len(terms) > 1:
+                terms = [terms[i] + terms[i + 1] for i in range(0, len(terms), 2)]
+            ahead.append(fresh[c] - terms[0])
         spread = [row_of(panel, j) for j in range(8)]
+        near = min(k + 1 + ND, 16)
+        if near < 16:
+            wide = [jnp.zeros((8, T), jnp.float32)] * 16
+            wide[k] = panel
+            away = dot(jnp.concatenate(rows[near:], axis=0), jnp.concatenate(wide, axis=0))
         for g in range(k + 1, 16):
             acc = jnp.where(inside, 0.0, rows[g])
-            for j in range(8):
-                acc = acc - cols[g - k][j] * spread[j]
+            if g < near:
+                for j in range(8):
+                    acc = acc - cols[g - k - 1][j] * spread[j]
+            else:
+                acc = acc - away[8 * (g - near):8 * (g - near) + 8]
             rows[g] = acc
     return out
 
 def solve_kernel(c_ref, x_ref, z_ref, a_ref, l_ref, v_ref):
     n = c_ref.shape[0]
     nb = n // T
+    wide = n + T
     for i in range(nb):
         for j in range(i, nb):
             a_ref[i * T:(i + 1) * T, j * T:(j + 1) * T] = 0.5 * (
                 c_ref[i * T:(i + 1) * T, j * T:(j + 1) * T] + c_ref[j * T:(j + 1) * T, i * T:(i + 1) * T].T)
-    a_ref[:, n:] = x_ref[...]
-
-    def step(k, _):
-        base = pl.multiple_of(k * T, T)
-        here = pl.ds(base, T)
-        rows = [a_ref[pl.ds(base + 8 * g, 8), here] for g in range(16)]
-        rows = factor(rows)
+    start = pl.multiple_of(lax.axis_index("cls") * T, T)
+    for i in range(nb):
+        here = slice(i * T, (i + 1) * T)
+        a_ref[here, n:] = (x_ref[:, here] + 0.5 * c_ref[pl.ds(start, T), here]).T - 0.5 * c_ref[here, pl.ds(start, T)]
+    def update(k, i):
+        here, there = slice(k * T, (k + 1) * T), slice(i * T, (i + 1) * T)
+        a_ref[there, i * T:] -= dot(v_ref[here, there], v_ref[here, i * T:], ((0,), (0,)))
+
+    for k in range(nb):
+        here = slice(k * T, (k + 1) * T)
+        rows = factor([a_ref[k * T + 8 * g:k * T + 8 * g + 8, here] for g in range(16)])
+        for i in range(k + 1, nb):
+            if k:
+                update(k - 1, i)
         for g in range(16):
-            l_ref[pl.ds(base + 8 * g, 8), :] = rows[g]
-        v_ref[here, :] = dot(l_ref[here, :], a_ref[here, :])
-        def trail(i, _):
-            at = pl.multiple_of(i * T, T)
-            a_ref[pl.ds(at, T), :] -= dot(v_ref[here, pl.ds(at, T)], v_ref[here, :], ((0,), (0,)))
-            return 0
-        lax.fori_loop(k + 1, nb, trail, 0)
-        return 0
-    lax.fori_loop(0, nb, step, 0)
-    def back(s, _):
-        j = nb - 1 - s
-        at = pl.multiple_of(j * T, T)
-        known = dot(l_ref[pl.ds(at, T), :], v_ref[pl.ds(at, T), n:], ((0,), (0,)))
-        z_ref[pl.ds(at, T), :] = known
-        def one(i, _):
-            to = pl.multiple_of(i * T, T)
-            v_ref[pl.ds(to, T), n:] -= dot(v_ref[pl.ds(to, T), pl.ds(at, T)], known)
-            return 0
-        lax.fori_loop(0, j, one, 0)
-        return 0
-    lax.fori_loop(0, nb, back, 0)
+            l_ref[k * T + 8 * g:k * T + 8 * g + 8, :] = rows[g]
+        v_ref[here, (k + 1) * T:] = dot(l_ref[here, :], a_ref[here, (k + 1) * T:])
+        if k + 1 < nb:
+            update(k, k + 1)
+    y = v_ref[:, n:]
+    for j in range(nb - 1, -1, -1):
+        here = slice(j * T, (j + 1) * T)
+        known = dot(l_ref[here, :], y[here], ((0,), (0,)))
+        z_ref[here, :] = known
+        if j:
+            y = y[:j * T] - dot(v_ref[:j * T, here], known)
 
 def solve(c, x):
     n = c.shape[0]
     return pl.pallas_call(
         solve_kernel,
-        out_shape=jax.ShapeDtypeStruct(x.shape, jnp.float32),
+        out_shape=jax.ShapeDtypeStruct((n, T), jnp.float32),
         in_specs=[pl.BlockSpec(memory_space=pltpu.VMEM)] * 2,
         out_specs=pl.BlockSpec(memory_space=pltpu.VMEM),
         scratch_shapes=[pltpu.VMEM((n, n + T), jnp.float32), pltpu.VMEM((n, T), jnp.float32),
                         pltpu.VMEM((n, n + T), jnp.float32)],
         compiler_params=pltpu.CompilerParams(vmem_limit_bytes=40 << 20),
     )(c, x)
+
+
 def body(seed_scores, tile_vals, tile_cols, tile_count, tile_scale):
     slots, weights = by_offset(tile_cols, tile_count, tile_scale)
     tiles = tile_vals.reshape(-1, T, T)
-    direction, misfit, imaged, high, ct, xt = find_direction(slots, weights, seed_scores, tiles)
-    all_imaged = lax.all_gather(imaged, "cls", axis=1, tiled=True)
-    full, xt = sum_and_share(ct, xt)
-    start = lax.axis_index("cls") * T
-    mine = lax.dynamic_slice_in_dim(full, start, T, 1)
-    own = lax.dynamic_slice_in_dim(full, start, T, 0)
-    rhs = (xt + 0.5 * (own - mine.T)).T
-    change = solve(full, rhs)
-    packed = change.astype(jnp.bfloat16)
-    mixed = sum(jnp.dot(high[n], packed[n * T:(n + 1) * T], preferred_element_type=jnp.float32) for n in range(high.shape[0]))
-    solution = direction + mixed
-    residual = misfit - jnp.dot(all_imaged, change, precision=HI)
-    return (solution, residual)
+    direction, misfit, parts, high, ct, xt = find_direction(slots, weights, seed_scores, tiles)
+    all_parts = lax.all_gather(parts, "cls", axis=1, tiled=True)
+    full, xs = sum_and_share(ct, xt)
+    change = solve(full, xs)
+    rows = direction.shape[0]
+    top = change.astype(jnp.bfloat16)
+    rest = (change - top.astype(jnp.float32)).astype(jnp.bfloat16)
+
+    def times(a, b):
+        return jnp.dot(a, b, preferred_element_type=jnp.float32)
+
+    mixed = sum(times(high[n], top[n * T:(n + 1) * T]) for n in range(high.shape[0]))
+    coarse, fine = all_parts[:rows], all_parts[rows:]
+    residual = misfit - (times(coarse, top) + (times(coarse, rest) + times(fine, top)))
+    return (direction + mixed, residual)
+
+
 def solution(mesh):
     return jax.shard_map(
         body,

time: 210 us -> 174 us (0.83); the launches traced: 210 us -> 171 us
  Pallas kernels: 174 us -> 143 us
  local copies, waits for them, and re-layouts: 7.14 us -> 2.2 us
  matrix products: 11 us -> 8.8 us
    pallas_call x1, Pallas kernels: 69.7 us -> 38.8 us  [solve(): pl.pallas_call(solve_kernel, out_shape=jax.ShapeDtypeStruct((n, T), jnp.f...]
    unnamed x8 -> x6, local copies, waits for them, and re-layouts: 5.32 us -> 1.84 us
    dot_general x9 -> x11, matrix products: 11 us -> 8.8 us  [times(): return jnp.dot(a, b, preferred_element_type=jnp.float32)]
  transfers between devices with their start and end apart: 1 -> 1, of which waited for: 0 -> 0; matrix products, arithmetic and copies ran while one was open for 3% -> 2% of each run, Pallas kernels for 53% -> 47%
where the time goes in v3:
time: 174 us; the launch traced here: 171 us
  Pallas kernels  143 us (82%)
  between operations  14.5 us (8%)
  matrix products  8.8 us (5%)
  local copies, waits for them, and re-layouts  2.2 us (1%)
  other arithmetic  1.87 us (1%)
    pallas_call x1, Pallas kernels, find_direction(): pl.pallas_call(direction_kernel, out_shape=[jax.ShapeDtypeStruct((rows, w...  63.9 us
    pallas_call x1, Pallas kernels, sum_and_share(): pl.pallas_call(sum_kernel, out_shape=[jax.ShapeDtypeStruct((4, 2) + cut,...  40.6 us
    pallas_call x1, Pallas kernels, solve(): pl.pallas_call(solve_kernel, out_shape=jax.ShapeDtypeStruct((n, T), jnp.f...  38.8 us
    dot_general x11, matrix products, times(): return jnp.dot(a, b, preferred_element_type=jnp.float32)  8.8 us
  transfers between devices with their start and end apart: 1, of which 0 were waited for; matrix products, arithmetic and copies ran while one was open for 2% of the time, Pallas kernels for 47%

profile of v3, /device:TPU:1, one launch (start us, length us, event | category | flops | bytes accessed | tf_op | source)
XLA Modules:
  0.0 170.7 jit_solution(4631604852223433011)
XLA Ops:
  7.2 0.0 all-gather.2.cloned.1.call-start
  7.3 0.8 add_select_fusion
  8.0 0.1 copy.7
  8.1 0.1 select_reduce_fusion.1
  8.3 0.1 reshape.58.slot_ref
  8.4 0.8 fusion.41
  9.1 0.1 copy.8
  9.2 0.1 select_reduce_fusion
  9.4 0.1 reshape.59.weight_ref
  9.5 0.0 copy-start
  9.5 1.1 copy-done
  10.6 63.9 %shard_map.68 = (f32[1536,128]{1,0:T(8,128)S(1)}, f32[1536,128]{1,0:T(8,128)S(1)}, bf16[3072,128]{1,0:T(8,128)(2,1)}, bf16[8,1536,128]{2,1,0:T(8,128)(2,1)}, f32...) custom-call(s32[204]{0:T(256)S(1)} %reshape.58.slot_ref, f32[204]{0:T(256)S(1)} %reshape.59.weight_ref, ...), custom_call_target="tpu_custom_call" | custom-call | tf_op jit(solution)/shard_map/pallas_call | solution.py:212
  74.5 0.0 all-gather.2.cloned.1.call-update
  74.5 40.6 %shard_map.69 = (f32[4,2,4,4,8,1024]{5,4,3,2,1,0:T(8,128)S(1)}, f32[4,4,8,1024]{3,2,1,0:T(8,128)S(1)}) custom-call(f32[4,4,8,1024]{3,2,1,0:T(8,128)S(1)} %bitcast.33, f32[4,4,8,1024]{3,2,1,0:T(8,128)S(1)} %bitcast.34), custom_call_target="tpu_custom_call" | custom-call | tf_op jit(solution)/shard_map/pallas_call | solution.py:353
  115.1 0.0 copy-start.2
  115.1 38.8 %shard_map.70 = f32[1024,128]{1,0:T(8,128)S(1)} custom-call(f32[1024,1024]{1,0:T(8,128)S(1)} %bitcast.31, f32[128,1024]{1,0:T(8,128)S(1)} %bitcast.32), custom_call_target="tpu_custom_call" | custom-call | tf_op jit(solution)/shard_map/pallas_call | solution.py:474
  154.0 0.0 copy-done.2
  154.0 0.2 fusion.23
  154.3 0.2 convolution_add_fusion.6
  154.5 0.2 convolution_add_fusion.5
  154.8 0.2 convolution_add_fusion.4
  155.0 0.2 convolution_add_fusion.3
  155.3 0.2 convolution_add_fusion.2
  155.5 0.2 convolution_add_fusion.1
  155.8 1.1 fusion.15
  156.9 0.0 all-gather.2.cloned.1.call-done
  156.9 0.0 copy-start.1
  156.9 3.0 %fusion = f32[1536,128]{1,0:T(8,128)S(1)} fusion(bf16[1024,128]{1,0:T(8,128)(2,1)S(1)} %convert_element_type.9, bf16[3072,1024]{1,0:T(8,128)(2,1)} %all-gather.2.cloned.1.call-done), kind=kOutput, calls=%fused_computation | convolution fusion | flops 402653184 | bytes 4194304 | tf_op jit(solution)/shard_map/dot_general | solution.py:497
  159.9 0.7 copy-done.1
  160.6 1.0 fusion.9
  161.7 1.9 %fusion.12 = f32[1536,128]{1,0:T(8,128)} fusion(f32[1536,128]{1,0:T(8,128)S(1)} %get-tuple-element.16, f32[1536,128]{1,0:T(8,128)S(1)} %fusion.9, bf16[1024,128]{1,0:T(8,128)(2,1)S(1)} %convert_element_type.9, bf16[3072,1024]{1,0:T(8,128)(2,1)S(1)} %copy-done.1), kind=kOutput, calls=%fused_computation.8 | convolution fusion | flops 403046400 | bytes 5767168 | tf_op jit(solution)/shard_map/dot_general | solution.py:497
  (4 shorter events, 0.0 us)
Async XLA Ops:
  7.2 149.7 %all-gather.2.cloned.1.call-start = ((), (), s32[]{:S(2)}) async-start(), calls=%async_computation | async-start | bytes 7077888 | tf_op jit(solution)/shard_map/all_gather | solution.py:489
  9.5 1.1 copy-start
  115.1 38.9 %copy-start.2 = (bf16[8,1536,128]{2,1,0:T(8,128)(2,1)S(1)}, bf16[8,1536,128]{2,1,0:T(8,128)(2,1)}, u32[]{:S(2)}) copy-start(bf16[8,1536,128]{2,1,0:T(8,128)(2,1)} %get-tuple-element.11) | copy-start | bytes 9437188
  156.9 3.7 %copy-start.1 = (bf16[3072,1024]{1,0:T(8,128)(2,1)S(1)}, bf16[3072,1024]{1,0:T(8,128)(2,1)}, u32[]{:S(2)}) copy-start(bf16[3072,1024]{1,0:T(8,128)(2,1)} %all-gather.2.cloned.1.call-done) | copy-start | bytes 18874372
Sparse Core Ops, SparseCore 0:
  74.7 42.7 all-gather.1
